TPU v7x, 256 devices: a whole 4x4x8 slice. The times are simulated.
256 devices in a mesh: gz: 64 (over x, z, core), gy: 4 (over y).
Axes of the slice: x: 4, y: 4, z: 8, core: 2. Of those that a mesh axis runs over, the one named last changes fastest.
Arguments:
- velocity: float32 [3, 128, 8, 128], P(None, 'gz', 'gy'), may hold values from -6 to 6
- slip: float32 [3, 131072], P(None, ('gz', 'gy')), may hold values from -6 to 6
- rate: float32 [131072], P(('gz', 'gy')), may hold values from 0.5 to 4
- owner: int32 [131072, 1], P(('gz', 'gy')), may hold values from 0 to 63; in each aligned block of 512 rows (0 to 511, 512 to 1023, ...) at most 16 rows name the same one
- cell: int32 [131072], P(('gz', 'gy')), may hold values from 0 to 511
- count: int32 [256], P(('gz', 'gy')), may hold values from 256 to 512
- w_in: bfloat16 [12, 1024], replicated, may hold values from -1.75 to 1.75
- b_in: float32 [1024], replicated, may hold values from -3 to 3
- w_mid: bfloat16 [1024, 1024], replicated, may hold values from -0.1875 to 0.1875
- b_mid: float32 [1024], replicated, may hold values from -3 to 3
- w_out: bfloat16 [1024, 6], replicated, may hold values from -0.1875 to 0.1875
- tau_bar: bfloat16 [6, 128, 8, 128], P(None, 'gz', 'gy'), may hold values from -1.5 to 1.5
Outputs:
- stress: float32 [6, 128, 8, 128], P(None, 'gz', 'gy')
- velocity_bar: float32 [3, 128, 8, 128], P(None, 'gz', 'gy')
- slip_bar: float32 [3, 131072], P(None, ('gz', 'gy'))
- rate_bar: float32 [131072], P(('gz', 'gy'))
- grad_w_in: float32 [12, 1024], replicated
- grad_b_in: float32 [1024], replicated
- grad_w_mid: float32 [1024, 1024], replicated
- grad_b_mid: float32 [1024], replicated
- grad_w_out: float32 [1024, 6], replicated
Inputs may be any that keep to these rules, and one draw needn't show every extreme that they name: Each particle's cell lies in the slab owner names, in the y-range of the particle's own device index along gy. Among the 512 slots of one device, at most 16 name the same slab, and that many do for some slab. The cell is flattened in the order z, y, x of the owner's block. The first count slots of a device are live, the others empty.
All inputs are finite; a program needn't handle non-finite values.
Results may differ from a plain program's by a relative error of at most 0.007.
Values sent between devices are 32-bit elements; how exact they have to be, the bound alone decides.
A program may use at most 64 MiB of HBM per device.

v0:
```python
import jax
import jax.numpy as jnp
from jax import lax
from jax.sharding import PartitionSpec as P


def with_halo(cells, sides, width):
    for axis, dim in sides:
        count = lax.axis_size(axis)
        head = lax.slice_in_dim(cells, 0, width, axis=dim)
        tail = lax.slice_in_dim(cells, cells.shape[dim] - width, cells.shape[dim], axis=dim)
        cells = jnp.concatenate(
            [
                lax.ppermute(tail, axis, [(i, (i + 1) % count) for i in range(count)]),
                cells,
                lax.ppermute(head, axis, [((i + 1) % count, i) for i in range(count)]),
            ],
            axis=dim,
        )
    return cells


def dsilu(value):
    sig = jax.nn.sigmoid(value)
    return sig * (1.0 + value * (1.0 - sig))


def deposit(forces, cell_row, ncells):
    block = min(512, ncells)
    count_blocks = ncells // block

    def deposit_one_block(index):
        start = index * block
        onehot = (
            cell_row[0][:, None] == start + jnp.arange(block, dtype=jnp.int32)[None, :]
        ).astype(jnp.float32)
        return jnp.dot(
            forces, onehot, precision=lax.Precision.HIGHEST, preferred_element_type=jnp.float32
        )

    pieces = lax.map(deposit_one_block, jnp.arange(count_blocks, dtype=jnp.int32))
    return pieces.transpose(1, 0, 2).reshape(forces.shape[0], ncells)


def collect(values, cell_row, ncells):
    block = min(512, ncells)
    count_blocks = ncells // block

    def collect_one_block(index, total):
        start = index * block
        onehot = (
            start + jnp.arange(block, dtype=jnp.int32)[:, None] == cell_row[0][None, :]
        ).astype(jnp.float32)
        return total + jnp.dot(
            values, onehot, precision=lax.Precision.HIGHEST, preferred_element_type=jnp.float32
        )

    init = jnp.zeros((values.shape[0], cell_row.shape[1]), jnp.float32)
    return lax.fori_loop(0, count_blocks, collect_one_block, init)


def roll_diff(field):
    return (jnp.roll(field, -1, 3) - jnp.roll(field, 1, 3)) * 0.5


def shards(velocity, slip, rate, owner, cell, count, w_in, b_in, w_mid, b_mid, w_out, tau_bar):
    nparts = slip.shape[1]
    slabs = lax.axis_size("gz")
    capacity = 2 * nparts // slabs
    width_all = slabs * capacity
    ncz, ncy, ncx = (velocity.shape[1], velocity.shape[2], velocity.shape[3])
    ncells = ncz * ncy * ncx
    padded = with_halo(velocity, (("gz", 1), ("gy", 2)), 1)
    core = padded[:, 1:-1, 1:-1]
    along_z = (padded[:, 2:, 1:-1] - padded[:, :-2, 1:-1]) * 0.5
    along_y = (padded[:, 1:-1, 2:] - padded[:, 1:-1, :-2]) * 0.5
    grads = jnp.stack([along_z, along_y, roll_diff(core)], 1).reshape(9, ncells)
    live = jnp.arange(nparts, dtype=jnp.int32) < count[0]
    force = jnp.where(live[None, :], rate[None, :] * slip, 0.0)
    owners = owner[:, 0]
    member = (owners[:, None] == jnp.arange(slabs, dtype=jnp.int32)[None, :]).astype(jnp.int32)
    before = jnp.cumsum(member, 0) - member
    position = jnp.sum(before * member, 1)
    slot = owners * capacity + position
    send_force = jnp.zeros((3, width_all), jnp.float32).at[:, slot].set(force)
    send_cell = jnp.full((1, width_all), -1, jnp.int32).at[0, slot].set(jnp.where(live, cell, -1))
    recv_force, recv_cell = (
        lax.all_to_all(send_force, "gz", split_axis=1, concat_axis=1, tiled=True),
        lax.all_to_all(send_cell, "gz", split_axis=1, concat_axis=1, tiled=True),
    )
    source = deposit(recv_force, recv_cell, ncells)
    feats = jnp.concatenate([grads, source], 0).astype(jnp.bfloat16)
    tbar = tau_bar.reshape(tau_bar.shape[0], ncells)
    pre1 = jnp.einsum("fh,fc->hc", w_in, feats, preferred_element_type=jnp.float32) + b_in[:, None]
    hidden_one = jax.nn.silu(pre1).astype(jnp.bfloat16)
    pre2 = (
        jnp.einsum("gh,gc->hc", w_mid, hidden_one, preferred_element_type=jnp.float32)
        + b_mid[:, None]
    )
    hidden_two = jax.nn.silu(pre2).astype(jnp.bfloat16)
    stress = jnp.einsum("ho,hc->oc", w_out, hidden_two, preferred_element_type=jnp.float32)
    grad_w_out = jnp.einsum("hc,oc->ho", hidden_two, tbar, preferred_element_type=jnp.float32)
    back_two = jnp.einsum("ho,oc->hc", w_out, tbar, preferred_element_type=jnp.float32)
    delta_two = (back_two * dsilu(pre2)).astype(jnp.bfloat16)
    grad_w_mid = jnp.einsum("gc,hc->gh", hidden_one, delta_two, preferred_element_type=jnp.float32)
    grad_b_mid = jnp.sum(delta_two.astype(jnp.float32), 1)
    back_one = jnp.einsum("gh,hc->gc", w_mid, delta_two, preferred_element_type=jnp.float32)
    delta_one = (back_one * dsilu(pre1)).astype(jnp.bfloat16)
    grad_w_in = jnp.einsum("fc,hc->fh", feats, delta_one, preferred_element_type=jnp.float32)
    grad_b_in = jnp.sum(delta_one.astype(jnp.float32), 1)
    grad_w_in, grad_b_in, grad_w_mid, grad_b_mid, grad_w_out = lax.psum(
        (grad_w_in, grad_b_in, grad_w_mid, grad_b_mid, grad_w_out), ("gz", "gy")
    )
    feats_bar = jnp.einsum("fh,hc->fc", w_in, delta_one, preferred_element_type=jnp.float32)
    grads_bar = feats_bar[:9].reshape(3, 3, ncz, ncy, ncx)
    joint = with_halo(grads_bar.reshape(9, ncz, ncy, ncx), (("gz", 1), ("gy", 2)), 1)
    joint = joint.reshape(3, 3, ncz + 2, ncy + 2, ncx)
    term_z = (joint[:, 0, 2:, 1:-1] - joint[:, 0, :-2, 1:-1]) * 0.5
    term_y = (joint[:, 1, 1:-1, 2:] - joint[:, 1, 1:-1, :-2]) * 0.5
    term_x = roll_diff(joint[:, 2, 1:-1, 1:-1])
    velocity_bar = -(term_z + term_y + term_x)
    source_bar = feats_bar[9:12]
    per_slot = collect(source_bar, recv_cell, ncells)
    returned = lax.all_to_all(per_slot, "gz", split_axis=1, concat_axis=1, tiled=True)
    at_particle = returned[:, slot]
    slip_bar = jnp.where(live[None, :], rate[None, :] * at_particle, 0.0)
    rate_bar = jnp.where(live, jnp.sum(slip * at_particle, 0), 0.0)
    return (
        stress.reshape(stress.shape[0], ncz, ncy, ncx),
        velocity_bar,
        slip_bar,
        rate_bar,
        grad_w_in,
        grad_b_in,
        grad_w_mid,
        grad_b_mid,
        grad_w_out,
    )


def solution(mesh):
    return jax.shard_map(
        shards,
        mesh=mesh,
        in_specs=(
            P(None, "gz", "gy", None),
            P(None, ("gz", "gy")),
            P(("gz", "gy")),
            P(("gz", "gy"), None),
            P(("gz", "gy")),
            P(("gz", "gy")),
            P(),
            P(),
            P(),
            P(),
            P(),
            P(None, "gz", "gy", None),
        ),
        out_specs=(
            P(None, "gz", "gy", None),
            P(None, "gz", "gy", None),
            P(None, ("gz", "gy")),
            P(("gz", "gy")),
            P(),
            P(),
            P(),
            P(),
            P(),
        ),
        check_vma=False,
    )
```

profile of v0, /device:TPU:2, one launch (start us, length us, event | category | flops | bytes accessed | tf_op | source)
XLA Modules:
  0.0 601.2 jit_solution(1143076900839981350)
XLA Ops:
  8.0 5.3 collective-permute-start
  14.7 1.2 reduce-window.6
  18.3 2.4 scatter_custom_fusion.1
  21.5 9.7 %all-to-all-start.1 = ((s32[1,64,16]{2,0,1:T(1,128)}), s32[1,64,16]{2,0,1:T(1,128)S(1)}, u32[]{:S(2)}, u32[]{:S(2)}) async-start(s32[1,64,16]{2,0,1:T(1,128)} %bitcast.14), calls=%async_computation.1 | async-start | bytes 65536 | tf_op jit(solution)/shard_map/all_to_all | solution.py:89
  34.8 3.1 collective-permute-start.2
  39.7 1.9 scatter_custom_fusion
  41.6 1.1 copy.79
  42.7 10.3 %all-to-all-start = ((f32[3,64,16]{2,0,1:T(4,128)}), f32[3,64,16]{2,0,1:T(4,128)S(1)}, u32[]{:S(2)}, u32[]{:S(2)}) async-start(f32[3,64,16]{2,0,1:T(4,128)} %copy.79), calls=%async_computation | async-start | bytes 262144 | tf_op jit(solution)/shard_map/all_to_all | solution.py:88
  54.7 7.7 %all-to-all-done = f32[3,64,16]{2,0,1:T(4,128)S(1)} async-done(((f32[3,64,16]{2,0,1:T(4,128)}), f32[3,64,16]{2,0,1:T(4,128)S(1)}, u32[]{:S(2)}, u32[]{:S(2)}) %all-to-all-start) | async-done | bytes 12320 | tf_op jit(solution)/shard_map/all_to_all | solution.py:88
  63.9 1.6 fusion.4
  66.7 1.6 convert_reduce_fusion
  68.3 2.4 convert_reduce_fusion.1
  71.1 0.9 fusion.29
  72.0 3.3 fusion.53
  77.5 3.3 collective-permute-start.5
  81.6 6.7 %all-to-all-start.2 = ((f32[3,64,16]{2,0,1:T(4,128)}), f32[3,64,16]{2,0,1:T(4,128)S(1)}, u32[]{:S(2)}, u32[]{:S(2)}) async-start(f32[3,64,16]{2,0,1:T(4,128)} %copy.86), calls=%async_computation.2 | async-start | bytes 262144 | tf_op jit(solution)/shard_map/all_to_all | solution.py:124
  89.1 2.7 collective-permute-start.7
  91.8 5.9 all-to-all-done.2
  98.2 1.0 gather_fusion
  101.8 212.4 %all-reduce.7.cloned.1.call-done = (f32[12,1024]{1,0:T(8,128)}, f32[1024]{0:T(1024)}, f32[1024]{0:T(1024)}, f32[1024,6]{0,1:T(8,128)}) async-done(((f32[12,1024]{1,0:T(8,128)}, f32[1024]{0:T(1024)}, f32[1024]{0:T(1024)}, f32[1024,6]{0,1:T(8,128)}), (f32[12,1024]{1,0:T(8,128)}, f32[1024]{0:T(1024)}, f32[1024]{0:T(1024)}, f32[1024,6]{0,1:T(8,128)})) %all-reduce.7.cloned.1.call-update) | async-done | bytes 81936 | tf_op jit(solution)/shard_map/psum | solution.py:111
  314.1 271.5 %all-reduce.5.cloned.1.call-done = f32[1024,1024]{1,0:T(8,128)} async-done(((f32[1024,1024]{1,0:T(8,128)}), f32[1024,1024]{1,0:T(8,128)}) %all-reduce.5.cloned.1.call-update) | async-done | bytes 4194320 | tf_op jit(solution)/shard_map/psum | solution.py:111
  585.6 1.5 copy.111
  587.1 1.3 copy.112
  588.4 4.8 copy.113
  (94 shorter events, 22.6 us)
Async XLA Ops:
  7.2 56.7 %copy-start = (bf16[1024,1024]{1,0:T(8,128)(2,1)S(1)}, bf16[1024,1024]{1,0:T(8,128)(2,1)}, u32[]{:S(2)}) copy-start(bf16[1024,1024]{1,0:T(8,128)(2,1)} %param.20) | copy-start | bytes 6291460
  8.0 26.0 %collective-permute-start = (f32[3,1,2,128]{3,2,1,0:T(2,128)S(1)}, f32[3,1,2,128]{3,2,1,0:T(2,128)S(1)}, u32[]{:S(2)}, u32[]{:S(2)}) collective-permute-start(f32[3,1,2,128]{3,2,1,0:T(2,128)S(1)} %get-tuple-element.90), channel_id=1, source_target_pairs={{4,0},{8,4},{12,8},{16,12},{20,16},{24,20},{28,24},{32,28},{36,32}... | collective-permute-start | bytes 9224 | tf_op jit(solution)/shard_map/ppermute | solution.py:16
  13.3 20.7 %collective-permute-start.1 = (f32[3,1,2,128]{3,2,1,0:T(2,128)S(1)}, f32[3,1,2,128]{3,2,1,0:T(2,128)S(1)}, u32[]{:S(2)}, u32[]{:S(2)}) collective-permute-start(f32[3,1,2,128]{3,2,1,0:T(2,128)S(1)} %get-tuple-element.91), channel_id=1, source_target_pairs={{0,4},{4,8},{8,12},{12,16},{16,20},{20,24},{24,28},{28,32},{32,36}... | collective-permute-start | bytes 9224 | tf_op jit(solution)/shard_map/ppermute | solution.py:14
  14.7 48.7 %copy-start.1 = (bf16[12,1024]{1,0:T(8,128)(2,1)S(1)}, bf16[12,1024]{1,0:T(8,128)(2,1)}, u32[]{:S(2)}) copy-start(bf16[12,1024]{1,0:T(8,128)(2,1)} %param.18) | copy-start | bytes 73732
  21.5 21.2 %all-to-all-start.1 = ((s32[1,64,16]{2,0,1:T(1,128)}), s32[1,64,16]{2,0,1:T(1,128)S(1)}, u32[]{:S(2)}, u32[]{:S(2)}) async-start(s32[1,64,16]{2,0,1:T(1,128)} %bitcast.14), calls=%async_computation.1 | async-start | bytes 65536 | tf_op jit(solution)/shard_map/all_to_all | solution.py:89
  34.8 19.8 %collective-permute-start.2 = (f32[3,4,1,128]{3,2,1,0:T(1,128)S(1)}, f32[3,4,1,128]{3,2,1,0:T(1,128)S(1)}, u32[]{:S(2)}, u32[]{:S(2)}) collective-permute-start(f32[3,4,1,128]{3,2,1,0:T(1,128)S(1)} %get-tuple-element.82), channel_id=1, source_target_pairs={{1,0},{2,1},{3,2},{0,3},{5,4},{6,5},{7,6},{4,7},{9,8},{10,9},{11,1... | collective-permute-start | bytes 18440 | tf_op jit(solution)/shard_map/ppermute | solution.py:16
  37.9 16.7 %collective-permute-start.3 = (f32[3,4,1,128]{3,2,1,0:T(1,128)S(1)}, f32[3,4,1,128]{3,2,1,0:T(1,128)S(1)}, u32[]{:S(2)}, u32[]{:S(2)}) collective-permute-start(f32[3,4,1,128]{3,2,1,0:T(1,128)S(1)} %get-tuple-element.83), channel_id=1, source_target_pairs={{0,1},{1,2},{2,3},{3,0},{4,5},{5,6},{6,7},{7,4},{8,9},{9,10},{10,1... | collective-permute-start | bytes 18440 | tf_op jit(solution)/shard_map/ppermute | solution.py:14
  41.6 22.3 %copy-start.6 = (f32[1024]{0:T(1024)S(1)}, f32[1024]{0:T(1024)}, u32[]{:S(2)}) copy-start(f32[1024]{0:T(1024)} %param.21) | copy-start | bytes 12292
  41.6 22.3 %copy-start.7 = (f32[1024]{0:T(1024)S(1)}, f32[1024]{0:T(1024)}, u32[]{:S(2)}) copy-start(f32[1024]{0:T(1024)} %param.19) | copy-start | bytes 12292
  42.7 19.7 %all-to-all-start = ((f32[3,64,16]{2,0,1:T(4,128)}), f32[3,64,16]{2,0,1:T(4,128)S(1)}, u32[]{:S(2)}, u32[]{:S(2)}) async-start(f32[3,64,16]{2,0,1:T(4,128)} %copy.79), calls=%async_computation | async-start | bytes 262144 | tf_op jit(solution)/shard_map/all_to_all | solution.py:88
  53.0 261.1 %all-reduce.7.cloned.1.call-start = ((), (), s32[]{:S(2)}) async-start(), calls=%async_computation.4 | async-start | bytes 212992 | tf_op jit(solution)/shard_map/psum | solution.py:111
  63.9 1.6 copy-start.3
  75.4 510.2 %all-reduce.5.cloned.1.call-start = ((), (), s32[]{:S(2)}) async-start(), calls=%async_computation.3 | async-start | bytes 8388608 | tf_op jit(solution)/shard_map/psum | solution.py:111
  75.5 23.8 %copy-start.4 = (f32[512]{0:T(512)S(1)}, f32[512]{0:T(512)}, u32[]{:S(2)}) copy-start(f32[512]{0:T(512)} %param.14) | copy-start | bytes 6148
  75.5 12.9 %collective-permute-start.4 = (f32[9,1,2,128]{3,2,1,0:T(2,128)S(1)}, f32[9,1,2,128]{3,2,1,0:T(2,128)S(1)}, u32[]{:S(2)}, u32[]{:S(2)}) collective-permute-start(f32[9,1,2,128]{3,2,1,0:T(2,128)S(1)} %get-tuple-element.81), channel_id=1, source_target_pairs={{0,4},{4,8},{8,12},{12,16},{16,20},{20,24},{24,28},{28,32},{32,36}... | collective-permute-start | bytes 27656 | tf_op jit(solution)/shard_map/ppermute | solution.py:14
  77.5 10.9 %collective-permute-start.5 = (f32[9,1,2,128]{3,2,1,0:T(2,128)S(1)}, f32[9,1,2,128]{3,2,1,0:T(2,128)S(1)}, u32[]{:S(2)}, u32[]{:S(2)}) collective-permute-start(f32[9,1,2,128]{3,2,1,0:T(2,128)S(1)} %get-tuple-element.80), channel_id=1, source_target_pairs={{4,0},{8,4},{12,8},{16,12},{20,16},{24,20},{28,24},{32,28},{36,32}... | collective-permute-start | bytes 27656 | tf_op jit(solution)/shard_map/ppermute | solution.py:16
  81.6 16.2 %all-to-all-start.2 = ((f32[3,64,16]{2,0,1:T(4,128)}), f32[3,64,16]{2,0,1:T(4,128)S(1)}, u32[]{:S(2)}, u32[]{:S(2)}) async-start(f32[3,64,16]{2,0,1:T(4,128)} %copy.86), calls=%async_computation.2 | async-start | bytes 262144 | tf_op jit(solution)/shard_map/all_to_all | solution.py:124
  88.4 12.4 %collective-permute-start.6 = (f32[9,4,1,128]{3,2,1,0:T(1,128)S(1)}, f32[9,4,1,128]{3,2,1,0:T(1,128)S(1)}, u32[]{:S(2)}, u32[]{:S(2)}) collective-permute-start(f32[9,4,1,128]{3,2,1,0:T(1,128)S(1)} %get-tuple-element.78), channel_id=1, source_target_pairs={{0,1},{1,2},{2,3},{3,0},{4,5},{5,6},{6,7},{7,4},{8,9},{9,10},{10,1... | collective-permute-start | bytes 55304 | tf_op jit(solution)/shard_map/ppermute | solution.py:14
  89.1 11.8 %collective-permute-start.7 = (f32[9,4,1,128]{3,2,1,0:T(1,128)S(1)}, f32[9,4,1,128]{3,2,1,0:T(1,128)S(1)}, u32[]{:S(2)}, u32[]{:S(2)}) collective-permute-start(f32[9,4,1,128]{3,2,1,0:T(1,128)S(1)} %get-tuple-element.79), channel_id=1, source_target_pairs={{1,0},{2,1},{3,2},{0,3},{5,4},{6,5},{7,6},{4,7},{9,8},{10,9},{11,1... | collective-permute-start | bytes 55304 | tf_op jit(solution)/shard_map/ppermute | solution.py:16
  588.4 4.8 copy-start.5
  588.4 5.4 copy-start.2
Sparse Core Ops, SparseCore 0:
  75.5 238.5 all-reduce.6
  320.2 265.3 all-reduce.4
where the time goes:
time: 602 us; the launch traced here: 601 us
  waiting for transfers between devices  498 us (83%)
  starting transfers between devices  42.2 us (7%)
  local copies, waits for them, and re-layouts  24.4 us (4%)
  between operations  15 us (2%)
  matrix products  13.5 us (2%)
  other arithmetic  8.1 us (1%)
    psum x2, waiting for transfers between devices, shards(): lax.psum((grad_w_in, grad_b_in, grad_w_mid, grad_b_mid, grad_w_out), ('gz...  484 us
    ppermute x4, starting transfers between devices, with_halo(): lax.ppermute(head, axis, [((i + 1) % count, i) for i in range(count)])  14.4 us
  transfers between devices with their start and end apart: 13, of which 4 were waited for; matrix products, arithmetic and copies ran while one was open for 4% of the time, Pallas kernels for 0%

commit v1 on v0

--- a/solution.py
+++ b/solution.py
@@ -2,6 +2,11 @@
 import jax.numpy as jnp
 from jax import lax
 from jax.sharding import PartitionSpec as P
+
+
+def one_after_other(array, one, other):
+    half = lax.psum(array, one)
+    return lax.psum(half, other)
 
 
 def with_halo(cells, sides, width):
@@ -108,8 +113,8 @@
     delta_one = (back_one * dsilu(pre1)).astype(jnp.bfloat16)
     grad_w_in = jnp.einsum("fc,hc->fh", feats, delta_one, preferred_element_type=jnp.float32)
     grad_b_in = jnp.sum(delta_one.astype(jnp.float32), 1)
-    grad_w_in, grad_b_in, grad_w_mid, grad_b_mid, grad_w_out = lax.psum(
-        (grad_w_in, grad_b_in, grad_w_mid, grad_b_mid, grad_w_out), ("gz", "gy")
+    grad_w_in, grad_b_in, grad_w_mid, grad_b_mid, grad_w_out = one_after_other(
+        (grad_w_in, grad_b_in, grad_w_mid, grad_b_mid, grad_w_out), "gz", "gy"
     )
     feats_bar = jnp.einsum("fh,hc->fc", w_in, delta_one, preferred_element_type=jnp.float32)
     grads_bar = feats_bar[:9].reshape(3, 3, ncz, ncy, ncx)

time: 602 us -> 603 us (level)
    psum x2 -> x4, waiting for transfers between devices: 484 us -> 479 us  [the longest x2 361 us: one_after_other(): half = lax.psum(array, one)]
  transfers between devices with their start and end apart: 13 -> 15, of which waited for: 4 -> 6; matrix products, arithmetic and copies ran while one was open for 4% -> 5% of each run, Pallas kernels for 0% -> 0%
where the time goes in v1:
time: 603 us; the launch traced here: 601 us
  waiting for transfers between devices  493 us (82%)
  starting transfers between devices  43.3 us (7%)
  local copies, waits for them, and re-layouts  25.5 us (4%)
  matrix products  16.5 us (3%)
  between operations  14.8 us (2%)
  other arithmetic  8.1 us (1%)
    psum x2, waiting for transfers between devices, one_after_other(): half = lax.psum(array, one)  361 us
    psum x2, waiting for transfers between devices, one_after_other(): return lax.psum(half, other)  119 us
    ppermute x4, starting transfers between devices, with_halo(): lax.ppermute(head, axis, [((i + 1) % count, i) for i in range(count)])  13.9 us
  transfers between devices with their start and end apart: 15, of which 6 were waited for; matrix products, arithmetic and copies ran while one was open for 5% of the time, Pallas kernels for 0%

profile of v1, /device:TPU:2, one launch (start us, length us, event | category | flops | bytes accessed | tf_op | source)
XLA Modules:
  0.0 601.2 jit_solution(1807877798245109083)
XLA Ops:
  8.1 5.3 collective-permute-start
  18.3 2.4 scatter_custom_fusion.1
  21.5 9.7 %all-to-all-start.1 = ((s32[1,64,16]{2,0,1:T(1,128)}), s32[1,64,16]{2,0,1:T(1,128)S(1)}, u32[]{:S(2)}, u32[]{:S(2)}) async-start(s32[1,64,16]{2,0,1:T(1,128)} %bitcast.14), calls=%async_computation.1 | async-start | bytes 65536 | tf_op jit(solution)/shard_map/all_to_all | solution.py:94
  34.8 3.1 collective-permute-start.2
  38.9 1.9 scatter_custom_fusion
  41.9 10.3 %all-to-all-start = ((f32[3,64,16]{2,0,1:T(4,128)}), f32[3,64,16]{2,0,1:T(4,128)S(1)}, u32[]{:S(2)}, u32[]{:S(2)}) async-start(f32[3,64,16]{2,0,1:T(4,128)} %copy.79), calls=%async_computation | async-start | bytes 262144 | tf_op jit(solution)/shard_map/all_to_all | solution.py:93
  53.9 7.7 %all-to-all-done = f32[3,64,16]{2,0,1:T(4,128)S(1)} async-done(((f32[3,64,16]{2,0,1:T(4,128)}), f32[3,64,16]{2,0,1:T(4,128)S(1)}, u32[]{:S(2)}, u32[]{:S(2)}) %all-to-all-start) | async-done | bytes 12320 | tf_op jit(solution)/shard_map/all_to_all | solution.py:93
  63.0 1.6 fusion.4
  65.5 1.6 convert_reduce_fusion
  67.1 2.3 convert_reduce_fusion.1
  71.4 5.2 fusion.53
  76.7 161.9 %all-reduce.12.cloned.1.call-done = (f32[12,1024]{1,0:T(8,128)}, f32[1024]{0:T(1024)}, f32[1024]{0:T(1024)}, f32[1024,6]{0,1:T(8,128)}) async-done(((f32[12,1024]{1,0:T(8,128)}, f32[1024]{0:T(1024)}, f32[1024]{0:T(1024)}, f32[1024,6]{0,1:T(8,128)}), (f32[12,1024]{1,0:T(8,128)}, f32[1024]{0:T(1024)}, f32[1024]{0:T(1024)}, f32[1024,6]{0,1:T(8,128)})) %all-reduce.12.cloned.1.call-update) | async-done | bytes 81936 | tf_op jit(solution)/shard_map/psum | solution.py:8
  238.6 198.9 %all-reduce.8.cloned.1.call-done = f32[1024,1024]{1,0:T(8,128)} async-done(((f32[1024,1024]{1,0:T(8,128)}), f32[1024,1024]{1,0:T(8,128)}) %all-reduce.8.cloned.1.call-update) | async-done | bytes 4194320 | tf_op jit(solution)/shard_map/psum | solution.py:8
  438.4 1.6 convolution_bitcast_fusion
  441.9 3.8 collective-permute-start.5
  446.5 7.4 %all-to-all-start.2 = ((f32[3,64,16]{2,0,1:T(4,128)}), f32[3,64,16]{2,0,1:T(4,128)S(1)}, u32[]{:S(2)}, u32[]{:S(2)}) async-start(f32[3,64,16]{2,0,1:T(4,128)} %copy.86), calls=%async_computation.2 | async-start | bytes 262144 | tf_op jit(solution)/shard_map/all_to_all | solution.py:129
  454.0 1.6 collective-permute-start.6
  455.6 1.8 collective-permute-start.7
  457.4 6.0 all-to-all-done.2
  467.3 17.4 %all-reduce.14.cloned.1.call-done = (f32[12,1024]{1,0:T(8,128)}, f32[1024]{0:T(1024)}, f32[1024]{0:T(1024)}, f32[1024,6]{0,1:T(8,128)}) async-done(((f32[12,1024]{1,0:T(8,128)}, f32[1024]{0:T(1024)}, f32[1024]{0:T(1024)}, f32[1024,6]{0,1:T(8,128)}), (f32[12,1024]{1,0:T(8,128)}, f32[1024]{0:T(1024)}, f32[1024]{0:T(1024)}, f32[1024,6]{0,1:T(8,128)})) %all-reduce.14.cloned.1.call-update) | async-done | bytes 81936 | tf_op jit(solution)/shard_map/psum | solution.py:9
  484.7 101.2 %all-reduce.10.cloned.1.call-done = f32[1024,1024]{1,0:T(8,128)} async-done(((f32[1024,1024]{1,0:T(8,128)}), f32[1024,1024]{1,0:T(8,128)}) %all-reduce.10.cloned.1.call-update) | async-done | bytes 4194320 | tf_op jit(solution)/shard_map/psum | solution.py:9
  585.9 1.5 copy.116
  587.4 1.3 copy.117
  588.7 4.8 copy.118
  (108 shorter events, 26.4 us)
Async XLA Ops:
  7.2 55.8 %copy-start = (bf16[1024,1024]{1,0:T(8,128)(2,1)S(1)}, bf16[1024,1024]{1,0:T(8,128)(2,1)}, u32[]{:S(2)}) copy-start(bf16[1024,1024]{1,0:T(8,128)(2,1)} %param.20) | copy-start | bytes 6291460
  7.2 55.3 %copy-start.3 = (bf16[12,1024]{1,0:T(8,128)(2,1)S(1)}, bf16[12,1024]{1,0:T(8,128)(2,1)}, u32[]{:S(2)}) copy-start(bf16[12,1024]{1,0:T(8,128)(2,1)} %param.18) | copy-start | bytes 73732
  8.1 25.9 %collective-permute-start = (f32[3,1,2,128]{3,2,1,0:T(2,128)S(1)}, f32[3,1,2,128]{3,2,1,0:T(2,128)S(1)}, u32[]{:S(2)}, u32[]{:S(2)}) collective-permute-start(f32[3,1,2,128]{3,2,1,0:T(2,128)S(1)} %get-tuple-element.94), channel_id=1, source_target_pairs={{4,0},{8,4},{12,8},{16,12},{20,16},{24,20},{28,24},{32,28},{36,32}... | collective-permute-start | bytes 9224 | tf_op jit(solution)/shard_map/ppermute | solution.py:21
  13.3 20.7 %collective-permute-start.1 = (f32[3,1,2,128]{3,2,1,0:T(2,128)S(1)}, f32[3,1,2,128]{3,2,1,0:T(2,128)S(1)}, u32[]{:S(2)}, u32[]{:S(2)}) collective-permute-start(f32[3,1,2,128]{3,2,1,0:T(2,128)S(1)} %get-tuple-element.95), channel_id=1, source_target_pairs={{0,4},{4,8},{8,12},{12,16},{16,20},{20,24},{24,28},{28,32},{32,36}... | collective-permute-start | bytes 9224 | tf_op jit(solution)/shard_map/ppermute | solution.py:19
  21.5 20.4 %all-to-all-start.1 = ((s32[1,64,16]{2,0,1:T(1,128)}), s32[1,64,16]{2,0,1:T(1,128)S(1)}, u32[]{:S(2)}, u32[]{:S(2)}) async-start(s32[1,64,16]{2,0,1:T(1,128)} %bitcast.14), calls=%async_computation.1 | async-start | bytes 65536 | tf_op jit(solution)/shard_map/all_to_all | solution.py:94
  34.8 18.9 %collective-permute-start.2 = (f32[3,4,1,128]{3,2,1,0:T(1,128)S(1)}, f32[3,4,1,128]{3,2,1,0:T(1,128)S(1)}, u32[]{:S(2)}, u32[]{:S(2)}) collective-permute-start(f32[3,4,1,128]{3,2,1,0:T(1,128)S(1)} %get-tuple-element.86), channel_id=1, source_target_pairs={{1,0},{2,1},{3,2},{0,3},{5,4},{6,5},{7,6},{4,7},{9,8},{10,9},{11,1... | collective-permute-start | bytes 18440 | tf_op jit(solution)/shard_map/ppermute | solution.py:21
  37.9 15.8 %collective-permute-start.3 = (f32[3,4,1,128]{3,2,1,0:T(1,128)S(1)}, f32[3,4,1,128]{3,2,1,0:T(1,128)S(1)}, u32[]{:S(2)}, u32[]{:S(2)}) collective-permute-start(f32[3,4,1,128]{3,2,1,0:T(1,128)S(1)} %get-tuple-element.87), channel_id=1, source_target_pairs={{0,1},{1,2},{2,3},{3,0},{4,5},{5,6},{6,7},{7,4},{8,9},{9,10},{10,1... | collective-permute-start | bytes 18440 | tf_op jit(solution)/shard_map/ppermute | solution.py:19
  40.7 22.3 %copy-start.9 = (f32[1024]{0:T(1024)S(1)}, f32[1024]{0:T(1024)}, u32[]{:S(2)}) copy-start(f32[1024]{0:T(1024)} %param.21) | copy-start | bytes 12292
  40.7 22.3 %copy-start.10 = (f32[1024]{0:T(1024)S(1)}, f32[1024]{0:T(1024)}, u32[]{:S(2)}) copy-start(f32[1024]{0:T(1024)} %param.19) | copy-start | bytes 12292
  41.9 19.7 %all-to-all-start = ((f32[3,64,16]{2,0,1:T(4,128)}), f32[3,64,16]{2,0,1:T(4,128)S(1)}, u32[]{:S(2)}, u32[]{:S(2)}) async-start(f32[3,64,16]{2,0,1:T(4,128)} %copy.79), calls=%async_computation | async-start | bytes 262144 | tf_op jit(solution)/shard_map/all_to_all | solution.py:93
  52.2 186.4 %all-reduce.12.cloned.1.call-start = ((), (), s32[]{:S(2)}) async-start(), calls=%async_computation.5 | async-start | bytes 212992 | tf_op jit(solution)/shard_map/psum | solution.py:8
  63.0 4.1 copy-start.2
  63.0 2.5 copy-start.6
  71.4 366.1 %all-reduce.8.cloned.1.call-start = ((), (), s32[]{:S(2)}) async-start(), calls=%async_computation.3 | async-start | bytes 8388608 | tf_op jit(solution)/shard_map/psum | solution.py:8
  76.7 408.1 %all-reduce.14.cloned.1.call-start = ((), (), s32[]{:S(2)}) async-start(), calls=%async_computation.6 | async-start | bytes 212992 | tf_op jit(solution)/shard_map/psum | solution.py:9
  238.6 347.3 %all-reduce.10.cloned.1.call-start = ((), (), s32[]{:S(2)}) async-start(), calls=%async_computation.4 | async-start | bytes 8388608 | tf_op jit(solution)/shard_map/psum | solution.py:9
  438.3 26.5 %copy-start.7 = (f32[512]{0:T(512)S(1)}, f32[512]{0:T(512)}, u32[]{:S(2)}) copy-start(f32[512]{0:T(512)} %param.14) | copy-start | bytes 6148
  440.0 13.9 %collective-permute-start.4 = (f32[9,1,2,128]{3,2,1,0:T(2,128)S(1)}, f32[9,1,2,128]{3,2,1,0:T(2,128)S(1)}, u32[]{:S(2)}, u32[]{:S(2)}) collective-permute-start(f32[9,1,2,128]{3,2,1,0:T(2,128)S(1)} %get-tuple-element.85), channel_id=1, source_target_pairs={{0,4},{4,8},{8,12},{12,16},{16,20},{20,24},{24,28},{28,32},{32,36}... | collective-permute-start | bytes 27656 | tf_op jit(solution)/shard_map/ppermute | solution.py:19
  441.9 12.1 %collective-permute-start.5 = (f32[9,1,2,128]{3,2,1,0:T(2,128)S(1)}, f32[9,1,2,128]{3,2,1,0:T(2,128)S(1)}, u32[]{:S(2)}, u32[]{:S(2)}) collective-permute-start(f32[9,1,2,128]{3,2,1,0:T(2,128)S(1)} %get-tuple-element.84), channel_id=1, source_target_pairs={{4,0},{8,4},{12,8},{16,12},{20,16},{24,20},{28,24},{32,28},{36,32}... | collective-permute-start | bytes 27656 | tf_op jit(solution)/shard_map/ppermute | solution.py:21
  446.5 16.8 %all-to-all-start.2 = ((f32[3,64,16]{2,0,1:T(4,128)}), f32[3,64,16]{2,0,1:T(4,128)S(1)}, u32[]{:S(2)}, u32[]{:S(2)}) async-start(f32[3,64,16]{2,0,1:T(4,128)} %copy.86), calls=%async_computation.2 | async-start | bytes 262144 | tf_op jit(solution)/shard_map/all_to_all | solution.py:129
  454.0 12.4 %collective-permute-start.6 = (f32[9,4,1,128]{3,2,1,0:T(1,128)S(1)}, f32[9,4,1,128]{3,2,1,0:T(1,128)S(1)}, u32[]{:S(2)}, u32[]{:S(2)}) collective-permute-start(f32[9,4,1,128]{3,2,1,0:T(1,128)S(1)} %get-tuple-element.82), channel_id=1, source_target_pairs={{0,1},{1,2},{2,3},{3,0},{4,5},{5,6},{6,7},{7,4},{8,9},{9,10},{10,1... | collective-permute-start | bytes 55304 | tf_op jit(solution)/shard_map/ppermute | solution.py:19
  455.6 10.8 %collective-permute-start.7 = (f32[9,4,1,128]{3,2,1,0:T(1,128)S(1)}, f32[9,4,1,128]{3,2,1,0:T(1,128)S(1)}, u32[]{:S(2)}, u32[]{:S(2)}) collective-permute-start(f32[9,4,1,128]{3,2,1,0:T(1,128)S(1)} %get-tuple-element.83), channel_id=1, source_target_pairs={{1,0},{2,1},{3,2},{0,3},{5,4},{6,5},{7,6},{4,7},{9,8},{10,9},{11,1... | collective-permute-start | bytes 55304 | tf_op jit(solution)/shard_map/ppermute | solution.py:21
  588.7 4.8 copy-start.8
  588.7 5.4 copy-start.5
  (3 other events, 4.1 us)
Sparse Core Ops, SparseCore 0:
  71.5 167.0 all-reduce.11
  242.7 194.7 all-reduce.7
  440.2 44.5 all-reduce.13
  486.9 98.9 all-reduce.9
